TPU v7x, 512 devices: a whole 4x8x8 slice. The times are simulated.
512 devices in a mesh: grp: 16 (over z, core), edge: 32 (over x, y).
Axes of the slice: x: 4, y: 8, z: 8, core: 2. Of those that a mesh axis runs over, the one named last changes fastest.
Arguments:
- grad_out: bfloat16 [65536, 256], P(('grp', 'edge')), may hold values from -6 to 6
- in_degree: int32 [65536], P(('grp', 'edge')), may hold values from 4 to 16
- w_self: bfloat16 [256, 256], replicated, may hold values from -0.375 to 0.375
- w_neigh: bfloat16 [256, 256], replicated, may hold values from -0.375 to 0.375
- block_dst_tile: int32 [131072], P(('grp', 'edge')), may hold values from 0 to 31
- block_src_group: int32 [131072], P(('grp', 'edge')), may hold values from 0 to 15
- edge_dst: int32 [131072, 128], P(('grp', 'edge')), may hold values from 0 to 127
- edge_src: int32 [131072, 128], P(('grp', 'edge')), may hold values from 0 to 127
- block_count: int32 [512], P(('grp', 'edge')), may hold values from 64 to 256, as said below
- mirror_tiles: int32 [512, 16], P(('grp', 'edge')), may hold values from 0 to 31
Outputs:
- grad_feats: bfloat16 [65536, 256], P(('grp', 'edge'))
- mirror_grads: bfloat16 [512, 16, 128, 256], P(('grp', 'edge'))
Inputs may be any that keep to these rules, and one draw needn't show every extreme that they name: The live slots of a device are its first block_count ones; in every group one device has all 256 slots live.
All inputs are finite; a program needn't handle non-finite values.
Results may differ from a plain program's by a relative error of at most 0.0043.
Values may be sent and summed in bfloat16 or wider, within the bound.
A program may use at most 64 MiB of HBM per device.

v0:
```python
import jax
import jax.numpy as jnp
from jax import lax
from jax.sharding import PartitionSpec as P


def block_terms(dst_tiles, rows_dst, rows_src, group_msg):
    lane_ids = jnp.arange(rows_dst.shape[1], dtype=jnp.int32)
    src_hot = (rows_src[:, :, None] == lane_ids).astype(jnp.bfloat16)
    dst_hot = (rows_dst[:, :, None] == lane_ids).astype(jnp.bfloat16)
    counts = jnp.einsum(
        "ber,bec->brc", src_hot, dst_hot, preferred_element_type=jnp.float32
    ).astype(jnp.bfloat16)
    msg_tiles = jnp.take(group_msg, dst_tiles, axis=0)
    return jnp.einsum("brc,bcd->brd", counts, msg_tiles, preferred_element_type=jnp.float32)


def per_device(
    grad_out,
    in_degree,
    w_self,
    w_neigh,
    block_dst_tile,
    block_src_group,
    edge_dst,
    edge_src,
    block_count,
    mirror_tiles,
):
    groups = lax.axis_size("grp")
    master_rows, features = grad_out.shape
    tile_rows = edge_dst.shape[1]
    blocks = edge_dst.shape[0]
    neigh_grad = jnp.dot(grad_out, w_neigh.T, preferred_element_type=jnp.float32)
    messages = (neigh_grad / in_degree.astype(jnp.float32)[:, None]).astype(jnp.bfloat16)
    group_msg = lax.all_gather(messages, "edge", axis=0, tiled=True)
    group_msg = group_msg.reshape(-1, tile_rows, features)
    live_count = block_count[0]
    live_mask = jnp.arange(blocks, dtype=jnp.int32) < live_count
    group_ids = jnp.arange(groups, dtype=jnp.int32)
    group_hot = ((block_src_group[:, None] == group_ids[None, :]) & live_mask[:, None]).astype(
        jnp.float32
    )

    def own_turn(step_index, mirror_sums):
        first_slot = step_index * 8
        terms = block_terms(
            lax.dynamic_slice_in_dim(block_dst_tile, first_slot, 8),
            lax.dynamic_slice_in_dim(edge_dst, first_slot, 8, 0),
            lax.dynamic_slice_in_dim(edge_src, first_slot, 8, 0),
            group_msg,
        )
        hot_turn = lax.dynamic_slice_in_dim(group_hot, first_slot, 8, 0)
        return mirror_sums + jnp.einsum(
            "bg,brd->grd", hot_turn, terms, precision=lax.Precision.HIGHEST
        )

    mirror = lax.fori_loop(
        0, (live_count + 7) // 8, own_turn, jnp.zeros((groups, tile_rows, features), jnp.float32)
    )
    relayed, tile_ids = (
        lax.all_to_all(mirror, "grp", split_axis=0, concat_axis=0, tiled=True),
        lax.all_to_all(mirror_tiles[0], "grp", split_axis=0, concat_axis=0, tiled=True),
    )
    tiles_group = group_msg.shape[0]
    tile_hot = (tile_ids[None, :] == jnp.arange(tiles_group, dtype=jnp.int32)[:, None]).astype(
        jnp.float32
    )
    group_dense = jnp.einsum("tg,grd->trd", tile_hot, relayed, precision=lax.Precision.HIGHEST)
    self_term = jnp.dot(grad_out, w_self.T, preferred_element_type=jnp.float32)
    own_sums = lax.psum_scatter(group_dense, "edge", scatter_dimension=0, tiled=True)
    grad_feats = (self_term + own_sums.reshape(master_rows, features)).astype(jnp.bfloat16)
    group_feats = lax.all_gather(grad_feats, "edge", axis=0, tiled=True)
    picked_tiles = jnp.take(group_feats.reshape(tiles_group, tile_rows, features), tile_ids, axis=0)
    mirror_grads = lax.all_to_all(picked_tiles, "grp", split_axis=0, concat_axis=0, tiled=True)
    return (grad_feats, mirror_grads[None])


def solution(mesh):
    placed = (
        P(("grp", "edge"), None),
        P(("grp", "edge")),
        P(),
        P(),
        P(("grp", "edge")),
        P(("grp", "edge")),
        P(("grp", "edge"), None),
        P(("grp", "edge"), None),
        P(("grp", "edge")),
        P(("grp", "edge"), None),
    )
    return jax.shard_map(
        per_device,
        mesh=mesh,
        in_specs=placed,
        out_specs=(P(("grp", "edge"), None), P(("grp", "edge"), None, None, None)),
        check_vma=False,
    )
```

profile of v0, /device:TPU:1, one launch (start us, length us, event | category | flops | bytes accessed | tf_op | source)
XLA Modules:
  0.0 781.6 jit_solution(12915878791726005174)
XLA Ops:
  8.1 1.7 fusion.16
  11.1 11.8 %all-to-all-start = ((s32[16,1,1]{2,1,0:T(1,128)}), s32[16,1,1]{2,1,0:T(1,128)S(1)}, u32[]{:S(2)}, u32[]{:S(2)}) async-start(s32[16,1,1]{2,1,0:T(1,128)} %copy.18), calls=%async_computation | async-start | bytes 16384 | tf_op jit(solution)/shard_map/all_to_all | solution.py:63
  24.4 72.4 %all-gather.3.cloned.1.call-done = bf16[4096,256]{1,0:T(8,128)(2,1)} async-done(((bf16[128,256]{1,0:T(8,128)(2,1)}), bf16[4096,256]{1,0:T(8,128)(2,1)}) %all-gather.3.cloned.1.call-update) | async-done | bytes 2097168 | tf_op jit(solution)/shard_map/all_gather | solution.py:36
  97.1 73.8 %while.10 = (s32[]{:T(128)}, f32[16,128,256]{2,0,1:T(8,128)S(1)}, s32[]{:T(128)}, f32[256,16]{1,0:T(8,128)S(1)}, s32[256,128]{1,0:T(8,128)}, /*index=5*/s32[256,...) while((s32[]{:T(128)}, f32[16,128,256]{2,0,1:T(8,128)S(1)}, ...), condition=%wide.region_1.2_spmd, body=%wide.region_0.1_spmd.sunk | while | flops 152175680 | bytes 7897407 | solution.py:58
  97.2 3.0 gather_fusion
  102.5 2.8 convolution_add_fusion.3
  105.4 3.0 gather_fusion
  110.7 2.8 convolution_add_fusion.3
  113.6 3.0 gather_fusion
  118.9 2.8 convolution_add_fusion.3
  121.8 3.0 gather_fusion
  127.1 2.8 convolution_add_fusion.3
  130.0 3.0 gather_fusion
  135.3 2.8 convolution_add_fusion.3
  138.2 3.0 gather_fusion
  143.5 2.8 convolution_add_fusion.3
  146.4 3.0 gather_fusion
  151.7 2.8 convolution_add_fusion.3
  154.6 3.0 gather_fusion
  159.9 2.8 convolution_add_fusion.3
  162.8 3.0 gather_fusion
  168.1 2.8 convolution_add_fusion.3
  170.9 2.6 copy.19
  173.5 93.8 %all-to-all-start.1 = ((f32[16,128,256]{2,1,0:T(8,128)}), f32[16,128,256]{2,1,0:T(8,128)S(1)}, u32[]{:S(2)}, u32[]{:S(2)}) async-start(f32[16,128,256]{2,1,0:T(8,128)} %copy.19), calls=%async_computation.1 | async-start | bytes 4194304 | tf_op jit(solution)/shard_map/all_to_all | solution.py:62
  267.8 48.5 %all-to-all-done.1 = f32[16,128,256]{2,1,0:T(8,128)S(1)} async-done(((f32[16,128,256]{2,1,0:T(8,128)}), f32[16,128,256]{2,1,0:T(8,128)S(1)}, u32[]{:S(2)}, u32[]{:S(2)}) %all-to-all-start.1) | async-done | bytes 2097184 | tf_op jit(solution)/shard_map/all_to_all | solution.py:62
  316.3 2.9 fusion.13
  319.2 4.4 copy.21
  323.7 320.6 %reduce-scatter.2.cloned.1.call-done = f32[1,128,256]{2,1,0:T(8,128)} async-done(((f32[32,128,256]{2,1,0:T(8,128)}), f32[1,128,256]{2,1,0:T(8,128)}) %reduce-scatter.2.cloned.1.call-update) | async-done | bytes 131088 | tf_op jit(solution)/shard_map/reduce_scatter | solution.py:71
  644.3 1.7 fusion.15
  646.1 85.4 %all-gather.5.cloned.1.call-done = bf16[4096,256]{1,0:T(8,128)(2,1)} async-done(((bf16[128,256]{1,0:T(8,128)(2,1)}), bf16[4096,256]{1,0:T(8,128)(2,1)}) %all-gather.5.cloned.1.call-update) | async-done | bytes 2097168 | tf_op jit(solution)/shard_map/all_gather | solution.py:73
  731.5 2.2 gather_fusion.1
  733.9 40.2 %all_to_all.22 = bf16[16,128,256]{2,1,0:T(8,128)(2,1)S(1)} all-to-all(bf16[16,128,256]{2,1,0:T(8,128)(2,1)S(1)} %broadcast_select_fusion), channel_id=1, replica_groups=mesh['grp'=16,'edge'=32] {'grp'}, dimensions={0} | all-to-all | bytes 2097152 | tf_op jit(solution)/shard_map/all_to_all | solution.py:75
  (62 shorter events, 26.2 us)
Async XLA Ops:
  7.2 0.9 copy-start
  7.2 89.9 %copy-start.3 = (s32[256]{0:T(256)S(1)}, s32[256]{0:T(256)}, u32[]{:S(2)}) copy-start(s32[256]{0:T(256)} %param.16) | copy-start | bytes 3076
  7.2 89.6 %all-gather.3.cloned.1.call-start = ((), (), s32[]{:S(2)}) async-start(), calls=%async_computation.4 | async-start | bytes 2162688 | tf_op jit(solution)/shard_map/all_gather | solution.py:36
  11.1 162.4 %all-to-all-start = ((s32[16,1,1]{2,1,0:T(1,128)}), s32[16,1,1]{2,1,0:T(1,128)S(1)}, u32[]{:S(2)}, u32[]{:S(2)}) async-start(s32[16,1,1]{2,1,0:T(1,128)} %copy.18), calls=%async_computation | async-start | bytes 16384 | tf_op jit(solution)/shard_map/all_to_all | solution.py:63
  173.5 142.8 %all-to-all-start.1 = ((f32[16,128,256]{2,1,0:T(8,128)}), f32[16,128,256]{2,1,0:T(8,128)S(1)}, u32[]{:S(2)}, u32[]{:S(2)}) async-start(f32[16,128,256]{2,1,0:T(8,128)} %copy.19), calls=%async_computation.1 | async-start | bytes 4194304 | tf_op jit(solution)/shard_map/all_to_all | solution.py:62
  267.3 377.0 %reduce-scatter.2.cloned.1.call-start = ((), (), s32[]{:S(2)}) async-start(), calls=%async_computation.5 | async-start | bytes 4325376 | tf_op jit(solution)/shard_map/reduce_scatter | solution.py:71
  323.6 320.7 %copy-start.1 = (bf16[256,256]{1,0:T(8,128)(2,1)S(1)}, bf16[256,256]{1,0:T(8,128)(2,1)}, u32[]{:S(2)}) copy-start(bf16[256,256]{1,0:T(8,128)(2,1)} %param.14) | copy-start | bytes 393220
  323.6 320.7 %copy-start.2 = (bf16[128,256]{1,0:T(8,128)(2,1)S(1)}, bf16[128,256]{1,0:T(8,128)(2,1)}, u32[]{:S(2)}) copy-start(bf16[128,256]{1,0:T(8,128)(2,1)} %param.12) | copy-start | bytes 196612
  323.6 407.9 %all-gather.5.cloned.1.call-start = ((), (), s32[]{:S(2)}) async-start(), calls=%async_computation.6 | async-start | bytes 2162688 | tf_op jit(solution)/shard_map/all_gather | solution.py:73
Sparse Core Ops, SparseCore 0:
  11.8 85.0 all-gather.2
  323.7 320.4 reduce-scatter.1
  648.5 82.9 all-gather.4
where the time goes:
time: 786 us; the launch traced here: 782 us
  waiting for transfers between devices  527 us (67%)
  starting transfers between devices  106 us (13%)
  matrix products  46 us (6%)
  local copies, waits for them, and re-layouts  44.9 us (6%)
  blocking collectives  40.2 us (5%)
  between operations  14.5 us (2%)
    reduce_scatter x1, waiting for transfers between devices, per_device(): lax.psum_scatter(group_dense, 'edge', scatter_dimension=0, tiled=True)  321 us
    all_to_all x1, starting transfers between devices, per_device(): lax.all_to_all(mirror, 'grp', split_axis=0, concat_axis=0, tiled=True)  93.8 us
    all_gather x1, waiting for transfers between devices, per_device(): group_feats = lax.all_gather(grad_feats, 'edge', axis=0, tiled=True)  85.4 us
    all_gather x1, waiting for transfers between devices, per_device(): group_msg = lax.all_gather(messages, 'edge', axis=0, tiled=True)  72.4 us
    all_to_all x1, waiting for transfers between devices, per_device(): lax.all_to_all(mirror, 'grp', split_axis=0, concat_axis=0, tiled=True)  48.5 us
    all_to_all x1, blocking collectives, per_device(): lax.all_to_all(picked_tiles, 'grp', split_axis=0, concat_axis=0, tiled=True)  40.2 us
    gather x9, local copies, waits for them, and re-layouts, block_terms(): msg_tiles = jnp.take(group_msg, dst_tiles, axis=0)  26.7 us
    dot_general x9, matrix products, own_turn(): jnp.einsum('bg,brd->grd', hot_turn, terms, precision=lax.Precision.HIGHEST)  25.6 us
  transfers between devices with their start and end apart: 5, of which 4 were waited for; matrix products, arithmetic and copies ran while one was open for 10% of the time, Pallas kernels for 0%

commit v1 on v0

v1 whole, which is shorter than its diff:
```python
import functools

import jax
import jax.numpy as jnp
from jax import lax
from jax.experimental import pallas as pl
from jax.experimental.pallas import tpu as pltpu
from jax.sharding import PartitionSpec as P

MESH = pl.DeviceIdType.MESH
NX, NY = 4, 8
NE = NX * NY
NG = 16
TILE = 128
D = 256
H = 128
B = 256
CHUNKS = 4
R = TILE // CHUNKS
MB = 1024 * 1024
F32 = jnp.float32
BF16 = jnp.bfloat16
NT = (((1,), (1,)), ((), ()))


def here():
    e = lax.axis_index("edge")
    return lax.div(e, NY), lax.rem(e, NY)


def wrap_x(x):
    return lax.rem(x + 2 * NX, NX)


def wrap_y(y):
    return lax.rem(y + 2 * NY, NY)


def node(x, y):
    return {"edge": wrap_x(x) * NY + wrap_y(y)}


def ring_peers():
    x, y = here()
    return [node(x + 1, y), node(x - 1, y), node(x, y + 1), node(x, y - 1)]


def greet(z_peers):
    barrier = pltpu.get_barrier_semaphore()
    for peer in ring_peers():
        pl.semaphore_signal(barrier, inc=1, device_id=peer, device_id_type=MESH)
    count = 4
    if z_peers:
        me = lax.axis_index("grp")

        def signal(i, carry):
            pl.semaphore_signal(
                barrier, inc=1, device_id={"grp": lax.rem(me + i, NG)}, device_id_type=MESH
            )
            return carry

        lax.fori_loop(1, NG, signal, 0)
        count += NG - 1
    pl.semaphore_wait(barrier, count)


def gather_copies(fa, fb, send, recv):
    x, y = here()
    rows = fa.shape[1]
    half_rows = rows // 2
    out = [[], []]
    for k in range(6):
        row_a, row_b = [], []
        for d, sign in enumerate((1, -1)):
            half = pl.ds(d * half_rows, half_rows)
            if k == 0:
                a = fa.at[pl.ds(y * NX + x, 1)]
            elif k == 1:
                a = fa.at[pl.ds(y * NX + wrap_x(x - sign), 1), half]
            elif k < 5:
                a = fa.at[pl.ds(wrap_y(y - (k - 2) * sign) * NX, NX)]
            else:
                a = fa.at[pl.ds(wrap_y(y - 3 * sign) * NX + d * (NX // 2), NX // 2)]
            to_a = node(x + sign, y) if k < 2 else node(x, y + sign)
            if k < 3:
                b = fb.at[pl.ds(x * NY + wrap_y(y - k * sign), 1)]
            elif k == 3:
                b = fb.at[pl.ds(x * NY + wrap_y(y - 3 * sign), 1), half]
            elif k == 4:
                b = fb.at[pl.ds(x * NY, NY)]
            else:
                b = fb.at[pl.ds(wrap_x(x - sign) * NY + d * (NY // 2), NY // 2)]
            to_b = node(x, y + sign) if k < 4 else node(x + sign, y)
            for color, ref, to, row in ((0, a, to_a, row_a), (1, b, to_b, row_b)):
                row.append(
                    pltpu.make_async_remote_copy(
                        src_ref=ref,
                        dst_ref=ref,
                        send_sem=send.at[color, k, d],
                        recv_sem=recv.at[color, k, d],
                        device_id=to,
                        device_id_type=MESH,
                    )
                )
        out[0].append(row_a)
        out[1].append(row_b)
    return out


def gather_stage(copies, stage):
    for color in range(2):
        if stage > 0:
            for c in copies[color][stage - 1]:
                c.wait_recv()
        if stage < 6:
            for c in copies[color][stage]:
                c.start()


def gather_finish(copies):
    for color in range(2):
        for row in copies[color]:
            for c in row:
                c.wait_send()


def gather_kernel(
    g_ref, deg_ref, w_ref, es_ref, ed_ref, mt_ref,
    ma_ref, mb_ref, counts_ref, ids_ref,
    held, send, recv, id_send, id_recv, out_sem,
):
    x, y = here()
    me = lax.axis_index("grp")
    ids_ref[pl.ds(me, 1)] = jnp.zeros((1, 8, 128), jnp.int32)
    ids_ref[pl.ds(me, 1), 0:1, 0:NG] = mt_ref[...].reshape(1, 1, NG)
    neigh = lax.dot_general(g_ref[...], w_ref[...], NT, preferred_element_type=F32)
    deg = jnp.broadcast_to(deg_ref[...].astype(F32), (TILE, TILE)).T
    ma_ref[pl.ds(y * NX + x, 1)] = (neigh[:, :H] / deg).astype(BF16)[None]
    mb_ref[pl.ds(x * NY + y, 1)] = (neigh[:, H:] / deg).astype(BF16)[None]
    greet(True)

    copies = gather_copies(ma_ref, mb_ref, send, recv)
    rows_id = lax.broadcasted_iota(jnp.int32, (TILE, TILE), 0)

    def id_copy(i):
        peer = lax.rem(me + i, NG)
        return pltpu.make_async_remote_copy(
            src_ref=ids_ref.at[pl.ds(me, 1)],
            dst_ref=ids_ref.at[pl.ds(me, 1)],
            send_sem=id_send.at[i],
            recv_sem=id_recv.at[i],
            device_id={"grp": peer},
            device_id_type=MESH,
        )

    def one(b):
        src = (rows_id == es_ref[pl.ds(b, 1), :]).astype(F32).astype(BF16)
        dst = (rows_id == ed_ref[pl.ds(b, 1), :]).astype(F32).astype(BF16)
        held[pl.ds(b, 1)] = lax.dot_general(
            src, dst, NT, preferred_element_type=F32
        ).astype(BF16)[None]

    per_part = B // 8

    def build(part):
        def body(i, carry):
            b = part * per_part + i * 4
            for j in range(4):
                one(b + j)
            return carry

        lax.fori_loop(0, per_part // 4, body, 0)
        span = pl.ds(part * per_part, per_part)
        copy = pltpu.make_async_copy(held.at[span], counts_ref.at[span], out_sem.at[part])
        copy.start()
        return copy

    outs = []
    for stage in range(7):
        gather_stage(copies, stage)
        if stage == 0:
            def start_id(i, carry):
                id_copy(i).start()
                return carry
            lax.fori_loop(1, NG, start_id, 0)
        if stage < 6:
            outs.append(build(stage))
        if stage in (1, 3):
            outs.append(build(6 + stage // 2))

    def end_id(i, carry):
        id_copy(i).wait()
        return carry

    lax.fori_loop(1, NG, end_id, 0)
    gather_finish(copies)
    for copy in outs:
        copy.wait()


def gather(grad_out, deg, w_neigh, edge_src, edge_dst, mirror_tiles):
    vmem = pl.BlockSpec(memory_space=pltpu.VMEM)
    return pl.pallas_call(
        gather_kernel,
        out_shape=(
            jax.ShapeDtypeStruct((NE, TILE, H), BF16),
            jax.ShapeDtypeStruct((NE, TILE, H), BF16),
            jax.ShapeDtypeStruct((B, TILE, TILE), BF16),
            jax.ShapeDtypeStruct((NG, 8, 128), jnp.int32),
        ),
        in_specs=[vmem] * 6,
        out_specs=(vmem, vmem, pl.BlockSpec(memory_space=pl.ANY), vmem),
        scratch_shapes=[
            pltpu.VMEM((B, TILE, TILE), BF16),
            pltpu.SemaphoreType.DMA((2, 6, 2)),
            pltpu.SemaphoreType.DMA((2, 6, 2)),
            pltpu.SemaphoreType.DMA((NG,)),
            pltpu.SemaphoreType.DMA((NG,)),
            pltpu.SemaphoreType.DMA((8,)),
        ],
        compiler_params=pltpu.CompilerParams(
            collective_id=0, has_side_effects=True, vmem_limit_bytes=32 * MB
        ),
        name="gather_messages",
    )(grad_out, deg, w_neigh, edge_src, edge_dst, mirror_tiles)


def sum_kernel(
    dt_ref, sg_ref, live_ref, ids_ref, counts_ref, ma_ref, mb_ref,
    part_ref, prev_ref, last_ref, tid_ref,
    held, head, size, nxt, sem,
):
    pieces = 8
    span = B // pieces
    copies = [
        pltpu.make_async_copy(
            counts_ref.at[pl.ds(p * span, span)], held.at[pl.ds(p * span, span)], sem.at[p]
        )
        for p in range(pieces)
    ]
    for c in copies:
        c.start()

    me = lax.axis_index("grp")

    def clear(t, carry):
        last_ref[t] = NG
        return carry

    lax.fori_loop(0, NE, clear, 0)

    def link(g, carry):
        t = ids_ref[g, 0, me]
        tid_ref[g] = t
        prev_ref[g] = last_ref[t]
        last_ref[t] = g
        return carry

    lax.fori_loop(0, NG, link, 0)

    def reset(s, carry):
        head[s] = 0
        size[s] = 0
        return carry

    lax.fori_loop(0, NG, reset, 0)

    def chain(b, carry):
        s = sg_ref[b]
        nxt[b] = head[s]
        head[s] = b
        size[s] = size[s] + 1
        return carry

    lax.fori_loop(0, live_ref[0], chain, 0)
    for c in copies:
        c.wait()

    def tile_of(b):
        t = dt_ref[b]
        ia = lax.rem(t, NY) * NX + lax.div(t, NY)
        return jnp.concatenate([ma_ref[ia], mb_ref[t]], axis=1)

    def group(s, carry):
        n = size[s]

        def pair(i, state):
            b1, acc = state
            b2 = nxt[b1]
            both = (2 * i + 1) < n
            second = jnp.where(both, held[b2], jnp.zeros((TILE, TILE), BF16))
            lhs = jnp.concatenate([held[b1], second], axis=1)
            rhs = jnp.concatenate([tile_of(b1), tile_of(b2)], axis=0)
            acc = acc + jnp.dot(lhs, rhs, preferred_element_type=F32)
            return nxt[b2], acc

        state = lax.fori_loop(
            0, lax.div(n + 1, 2), pair, (head[s], jnp.zeros((TILE, D), F32))
        )
        acc = state[1].astype(BF16)
        for c in range(CHUNKS):
            for h in range(2):
                part_ref[c, s, h] = acc[c * R : (c + 1) * R, h * H : (h + 1) * H]
        return carry

    lax.fori_loop(0, NG, group, 0)


def edge_sums(dst_tile, src_group, count, ids, counts, ma, mb):
    smem = pl.BlockSpec(memory_space=pltpu.SMEM)
    vmem = pl.BlockSpec(memory_space=pltpu.VMEM)
    return pl.pallas_call(
        sum_kernel,
        out_shape=(
            jax.ShapeDtypeStruct((CHUNKS, NG, 2, R, H), BF16),
            jax.ShapeDtypeStruct((NG,), jnp.int32),
            jax.ShapeDtypeStruct((NE,), jnp.int32),
            jax.ShapeDtypeStruct((NG,), jnp.int32),
        ),
        in_specs=[smem] * 4 + [pl.BlockSpec(memory_space=pl.ANY), vmem, vmem],
        out_specs=(vmem, smem, smem, smem),
        scratch_shapes=[
            pltpu.VMEM((B, TILE, TILE), BF16),
            pltpu.SMEM((NG,), jnp.int32),
            pltpu.SMEM((NG,), jnp.int32),
            pltpu.SMEM((B,), jnp.int32),
            pltpu.SemaphoreType.DMA((8,)),
        ],
        compiler_params=pltpu.CompilerParams(vmem_limit_bytes=32 * MB),
        name="edge_sums",
    )(dst_tile, src_group, count, ids, counts, ma, mb)


Z_ORDER = (8, 9, 7, 6, 10, 5, 11, 4, 12, 3, 13, 2, 14, 1, 15)


def merge_kernel(
    part_ref, prev_ref, last_ref, tid_ref, g_ref, w_ref,
    gf_ref, mg_ref,
    self_term, own_sem, z_send, z_recv, r_send, r_recv, f_send, f_recv, b_send, b_recv,
    *bufs,
):
    x, y = here()
    me = lax.axis_index("grp")
    names = (
        "relay", "sums", "sa0", "sa", "ra0", "ra", "ua", "ra4", "sa5", "ra5",
        "sb0", "sb1", "rb0", "rb1", "ub", "rb2", "sb", "rb", "fa", "fb", "picked",
    )
    per = len(names)
    chunks = [dict(zip(names, bufs[c * per : (c + 1) * per])) for c in range(CHUNKS)]

    greet(True)

    def z_copy(c, i):
        peer = lax.rem(me + i, NG)
        return pltpu.make_async_remote_copy(
            src_ref=part_ref.at[c, peer],
            dst_ref=chunks[c]["relay"].at[me],
            send_sem=z_send.at[c, i],
            recv_sem=z_recv.at[c, i],
            device_id={"grp": peer},
            device_id_type=MESH,
        )

    def own_copy(c):
        return pltpu.make_async_copy(
            part_ref.at[c, me], chunks[c]["relay"].at[me], own_sem.at[c]
        )

    for c in range(CHUNKS):
        own_copy(c).start()
        for i in Z_ORDER:
            z_copy(c, i).start()

    self_term[...] = lax.dot_general(g_ref[...], w_ref[...], NT, preferred_element_type=F32)

    def ring(c, color, k, d, src, dst):
        sign = 1 - 2 * d
        along_y = (k < 4) if color == 0 else (k >= 2)
        return pltpu.make_async_remote_copy(
            src_ref=src,
            dst_ref=dst,
            send_sem=r_send.at[c, color, k, d],
            recv_sem=r_recv.at[c, color, k, d],
            device_id=node(x, y + sign) if along_y else node(x + sign, y),
            device_id_type=MESH,
        )

    half_rows = R // 2

    def ring_copy(c, color, k, d):
        buf = chunks[c]
        half = pl.ds(d * half_rows, half_rows)
        if color == 0:
            if k == 0:
                src, dst = buf["sa0"].at[d], buf["ra0"].at[d]
            elif k < 4:
                src, dst = buf["sa"].at[k - 1, d], buf["ra"].at[k - 1, d]
            elif k == 4:
                src, dst = buf["ua"].at[wrap_x(x + 2), half], buf["ra4"].at[d]
            else:
                src, dst = buf["sa5"].at[d], buf["ra5"].at[d]
        else:
            if k == 0:
                src, dst = buf["sb0"].at[d], buf["rb0"].at[d]
            elif k == 1:
                src, dst = buf["sb1"].at[d], buf["rb1"].at[d]
            elif k == 2:
                src, dst = buf["ub"].at[wrap_y(y + 4), half], buf["rb2"].at[d]
            else:
                src, dst = buf["sb"].at[k - 3, d], buf["rb"].at[k - 3, d]
        return ring(c, color, k, d, src, dst)

    def tile_sum(c, color, xx, yy):
        return chunks[c]["sums"][last_ref[xx * NY + yy], color]

    def relay_stage(c):
        buf = chunks[c]
        own_copy(c).wait()

        def arrive(i, carry):
            z_copy(c, i).wait_recv()
            return carry

        lax.fori_loop(1, NG, arrive, 0)
        buf["sums"][NG] = jnp.zeros((2, R, H), F32)

        def add(g, carry):
            buf["sums"][g] = buf["relay"][g].astype(F32) + buf["sums"][prev_ref[g]]
            return carry

        for g in range(NG):
            add(g, 0)

    def reduce_a(c, k):
        buf = chunks[c]
        if k > 0:
            for d in range(2):
                ring_copy(c, 0, k - 1, d).wait_recv()
        if k == 0:
            for d in range(2):
                for j in range(2):
                    buf["sa0"][d, j] = tile_sum(c, 0, 2 * d + j, wrap_y(y + 4)).astype(BF16)
        elif k < 4:
            for d in range(2):
                yy = wrap_y(y + (4 - k) * (1 - 2 * d))
                for xx in range(NX):
                    v = tile_sum(c, 0, xx, yy)
                    if k > 1:
                        v = v + buf["ra"][k - 2, d, xx].astype(F32)
                    elif xx // 2 == d:
                        v = v + buf["ra0"][d, xx % 2].astype(F32)
                    buf["sa"][k - 1, d, xx] = v.astype(BF16)
        elif k == 4:
            for xx in range(NX):
                buf["ua"][xx] = (
                    tile_sum(c, 0, xx, y)
                    + buf["ra"][2, 0, xx].astype(F32)
                    + buf["ra"][2, 1, xx].astype(F32)
                )
        elif k == 5:
            for d in range(2):
                xx = wrap_x(x + 1 - 2 * d)
                buf["sa5"][d] = buf["ua"][xx]
                half = pl.ds(d * half_rows, half_rows)
                buf["sa5"][d, half] = buf["sa5"][d, half] + buf["ra4"][d]
        else:
            return buf["ua"][x] + buf["ra5"][0] + buf["ra5"][1]
        for d in range(2):
            ring_copy(c, 0, k, d).start()
        return None

    def reduce_b(c, k):
        buf = chunks[c]
        if k > 0:
            for d in range(2):
                ring_copy(c, 1, k - 1, d).wait_recv()
        if k == 0:
            for d in range(2):
                for j in range(4):
                    buf["sb0"][d, j] = tile_sum(c, 1, wrap_x(x + 2), 4 * d + j).astype(BF16)
        elif k == 1:
            for d in range(2):
                xx = wrap_x(x + 1 - 2 * d)
                for yy in range(NY):
                    v = tile_sum(c, 1, xx, yy)
                    if yy // 4 == d:
                        v = v + buf["rb0"][d, yy % 4].astype(F32)
                    buf["sb1"][d, yy] = v.astype(BF16)
        elif k == 2:
            for yy in range(NY):
                buf["ub"][yy] = (
                    tile_sum(c, 1, x, yy)
                    + buf["rb1"][0, yy].astype(F32)
                    + buf["rb1"][1, yy].astype(F32)
                )
        elif k < 6:
            for d in range(2):
                yy = wrap_y(y + (6 - k) * (1 - 2 * d))
                if k == 3:
                    buf["sb"][0, d] = buf["ub"][yy]
                    half = pl.ds(d * half_rows, half_rows)
                    buf["sb"][0, d, half] = buf["sb"][0, d, half] + buf["rb2"][d]
                else:
                    buf["sb"][k - 3, d] = buf["ub"][yy] + buf["rb"][k - 4, d]
        else:
            return buf["ub"][y] + buf["rb"][2, 0] + buf["rb"][2, 1]
        for d in range(2):
            ring_copy(c, 1, k, d).start()
        return None

    gathers = [
        gather_copies(chunks[c]["fa"], chunks[c]["fb"], f_send.at[c], f_recv.at[c])
        for c in range(CHUNKS)
    ]

    def back_copy(c, i):
        peer = lax.rem(me + i, NG)
        return pltpu.make_async_remote_copy(
            src_ref=chunks[c]["picked"].at[peer],
            dst_ref=mg_ref.at[0, me, pl.ds(c * R, R)],
            send_sem=b_send.at[c, i],
            recv_sem=b_recv.at[c, i],
            device_id={"grp": peer},
            device_id_type=MESH,
        )

    def back_own(c):
        return pltpu.make_async_copy(
            chunks[c]["picked"].at[me], mg_ref.at[0, me, pl.ds(c * R, R)], own_sem.at[CHUNKS + c]
        )

    def finish_tile(c):
        buf = chunks[c]
        own_a = reduce_a(c, 6)
        own_b = reduce_b(c, 6)
        rows = pl.ds(c * R, R)
        out_a = (self_term[rows, 0:H] + own_a).astype(BF16)
        out_b = (self_term[rows, H:D] + own_b).astype(BF16)
        gf_ref[rows, 0:H] = out_a
        gf_ref[rows, H:D] = out_b
        buf["fa"][pl.ds(y * NX + x, 1)] = out_a[None]
        buf["fb"][pl.ds(x * NY + y, 1)] = out_b[None]
        gather_stage(gathers[c], 0)

    def send_back(c):
        buf = chunks[c]
        gather_stage(gathers[c], 6)
        for g in range(NG):
            t = tid_ref[g]
            ia = lax.rem(t, NY) * NX + lax.div(t, NY)
            buf["picked"][g, :, 0:H] = buf["fa"][ia]
            buf["picked"][g, :, H:D] = buf["fb"][t]
        back_own(c).start()
        for i in Z_ORDER:
            back_copy(c, i).start()

    stages = []
    for k in range(6):
        def reduce_step(c, k=k):
            if k == 0:
                relay_stage(c)
            reduce_a(c, k)
            reduce_b(c, k)
        stages.append(reduce_step)
    stages.append(finish_tile)
    for k in range(1, 6):
        stages.append(lambda c, k=k: gather_stage(gathers[c], k))
    stages.append(send_back)

    lag = 3
    for tick in range(len(stages) + lag * (CHUNKS - 1)):
        for c in range(CHUNKS):
            k = tick - lag * c
            if 0 <= k < len(stages):
                stages[k](c)

    for c in range(CHUNKS):
        back_own(c).wait()

        def end(i, carry, c=c):
            z_copy(c, i).wait_send()
            back_copy(c, i).wait()
            return carry

        lax.fori_loop(1, NG, end, 0)
        for color in range(2):
            for k in range(6):
                for d in range(2):
                    ring_copy(c, color, k, d).wait_send()
        gather_finish(gathers[c])


def merge(part, prev, last, tid, grad_out, w_self):
    smem = pl.BlockSpec(memory_space=pltpu.SMEM)
    vmem = pl.BlockSpec(memory_space=pltpu.VMEM)
    hbm = pl.BlockSpec(memory_space=pl.ANY)
    half = R // 2
    per_chunk = [
        pltpu.VMEM((NG, 2, R, H), BF16),
        pltpu.VMEM((NG + 1, 2, R, H), F32),
        pltpu.VMEM((2, 2, R, H), BF16),
        pltpu.VMEM((3, 2, NX, R, H), BF16),
        pltpu.VMEM((2, 2, R, H), BF16),
        pltpu.VMEM((3, 2, NX, R, H), BF16),
        pltpu.VMEM((NX, R, H), F32),
        pltpu.VMEM((2, half, H), F32),
        pltpu.VMEM((2, R, H), F32),
        pltpu.VMEM((2, R, H), F32),
        pltpu.VMEM((2, 4, R, H), BF16),
        pltpu.VMEM((2, NY, R, H), BF16),
        pltpu.VMEM((2, 4, R, H), BF16),
        pltpu.VMEM((2, NY, R, H), BF16),
        pltpu.VMEM((NY, R, H), F32),
        pltpu.VMEM((2, half, H), F32),
        pltpu.VMEM((3, 2, R, H), F32),
        pltpu.VMEM((3, 2, R, H), F32),
        pltpu.VMEM((NE, R, H), BF16),
        pltpu.VMEM((NE, R, H), BF16),
        pltpu.VMEM((NG, R, D), BF16),
    ]
    dma = pltpu.SemaphoreType.DMA
    return pl.pallas_call(
        merge_kernel,
        out_shape=(
            jax.ShapeDtypeStruct((TILE, D), BF16),
            jax.ShapeDtypeStruct((1, NG, TILE, D), BF16),
        ),
        in_specs=[hbm, smem, smem, smem, vmem, vmem],
        out_specs=(vmem, hbm),
        scratch_shapes=[
            pltpu.VMEM((TILE, D), F32),
            dma((2 * CHUNKS,)),
            dma((CHUNKS, NG)),
            dma((CHUNKS, NG)),
            dma((CHUNKS, 2, 6, 2)),
            dma((CHUNKS, 2, 6, 2)),
            dma((CHUNKS, 2, 6, 2)),
            dma((CHUNKS, 2, 6, 2)),
            dma((CHUNKS, NG)),
            dma((CHUNKS, NG)),
        ]
        + per_chunk * CHUNKS,
        compiler_params=pltpu.CompilerParams(
            collective_id=1, has_side_effects=True, vmem_limit_bytes=32 * MB
        ),
        name="merge_mirrors",
    )(part, prev, last, tid, grad_out, w_self)


def per_device(
    grad_out,
    in_degree,
    w_self,
    w_neigh,
    block_dst_tile,
    block_src_group,
    edge_dst,
    edge_src,
    block_count,
    mirror_tiles,
):
    ma, mb, counts, ids = gather(
        grad_out, in_degree.reshape(1, -1), w_neigh, edge_src, edge_dst, mirror_tiles
    )
    part, prev, last, tid = edge_sums(
        block_dst_tile, block_src_group, block_count, ids, counts, ma, mb
    )
    return merge(part, prev, last, tid, grad_out, w_self)


def solution(mesh):
    placed = (
        P(("grp", "edge"), None),
        P(("grp", "edge")),
        P(),
        P(),
        P(("grp", "edge")),
        P(("grp", "edge")),
        P(("grp", "edge"), None),
        P(("grp", "edge"), None),
        P(("grp", "edge")),
        P(("grp", "edge"), None),
    )
    return jax.shard_map(
        per_device,
        mesh=mesh,
        in_specs=placed,
        out_specs=(P(("grp", "edge"), None), P(("grp", "edge"), None, None, None)),
        check_vma=False,
    )
```

time: 786 us -> 184 us (0.23)
  waiting for transfers between devices: 527 us -> 0 us
  Pallas kernels: 0 us -> 174 us
  starting transfers between devices: 106 us -> 0 us
  matrix products: 46 us -> 0 us
  blocking collectives: 40.2 us -> 0 us
  local copies, waits for them, and re-layouts: 44.9 us -> 7.81 us
  between operations: 14.5 us -> 1.33 us
    reduce_scatter x1 -> x0, waiting for transfers between devices: 321 us -> none  [per_device(): lax.psum_scatter(group_dense, 'edge', scatter_dimension=0, tiled=True)]
    pallas_call x0 -> x3, Pallas kernels: none -> 174 us  [the longest x1 122 us: merge(): pl.pallas_call(merge_kernel, out_shape=(jax.ShapeDtypeStruct((TILE, D), B...]
    all_gather x2 -> x0, waiting for transfers between devices: 158 us -> none  [the longest x1 85.4 us: per_device(): group_feats = lax.all_gather(grad_feats, 'edge', axis=0, tiled=True)]
    all_to_all x2 -> x0, starting transfers between devices: 106 us -> none  [the longest x1 93.8 us: per_device(): lax.all_to_all(mirror, 'grp', split_axis=0, concat_axis=0, tiled=True)]
    all_to_all x2 -> x0, waiting for transfers between devices: 48.5 us -> none  [the longest x1 48.5 us: per_device(): lax.all_to_all(mirror, 'grp', split_axis=0, concat_axis=0, tiled=True)]
    dot_general x21 -> x0, matrix products: 46 us -> none  [the longest x9 25.6 us: own_turn(): jnp.einsum('bg,brd->grd', hot_turn, terms, precision=lax.Precision.HIGHEST)]
    all_to_all x1 -> x0, blocking collectives: 40.2 us -> none  [per_device(): lax.all_to_all(picked_tiles, 'grp', split_axis=0, concat_axis=0, tiled=True)]
    gather x10 -> x0, local copies, waits for them, and re-layouts: 28.9 us -> none  [the longest x9 26.7 us: block_terms(): msg_tiles = jnp.take(group_msg, dst_tiles, axis=0)]
  transfers between devices with their start and end apart: 5 -> 0, of which waited for: 4 -> 0; matrix products, arithmetic and copies ran while one was open for 10% -> 0% of each run, Pallas kernels for 0% -> 0%
where the time goes in v1:
time: 184 us; the launch traced here: 183 us
  Pallas kernels  174 us (95%)
  local copies, waits for them, and re-layouts  7.81 us (4%)
    pallas_call x1, Pallas kernels, merge(): pl.pallas_call(merge_kernel, out_shape=(jax.ShapeDtypeStruct((TILE, D), B...  122 us
    pallas_call x1, Pallas kernels, gather(): pl.pallas_call(gather_kernel, out_shape=(jax.ShapeDtypeStruct((NE, TILE,...  40.1 us
    pallas_call x1, Pallas kernels, edge_sums(): pl.pallas_call(sum_kernel, out_shape=(jax.ShapeDtypeStruct((CHUNKS, NG, 2...  11.6 us
    unnamed x20, local copies, waits for them, and re-layouts  7.81 us

profile of v1, /device:TPU:1, one launch (start us, length us, event | category | flops | bytes accessed | tf_op | source)
XLA Modules:
  0.0 183.2 jit_solution(12608348070840032648)
XLA Ops:
  1.3 0.0 copy-start
  1.3 0.8 copy-done
  2.1 0.0 copy-start.1
  2.1 0.9 copy-done.1
  3.0 0.0 copy-start.2
  3.0 0.9 copy-done.2
  3.9 0.0 copy-start.3
  3.9 0.9 copy-done.3
  4.8 0.0 copy-start.7
  4.8 0.7 copy-done.7
  5.5 0.0 copy-start.8
  5.5 0.7 copy-done.8
  6.1 0.0 copy-start.4
  6.1 40.1 %gather_messages.1 = (bf16[32,128,128]{2,1,0:T(8,128)(2,1)S(1)}, bf16[32,128,128]{2,1,0:T(8,128)(2,1)S(1)}, bf16[256,128,128]{2,1,0:T(8,128)(2,1)S(1)}, s32[16,8,128]{2,1,0:T(8,128)S(1)}) custom-call(bf16[128,256]{1,0:T(8,128)(2,1)S(1)} %copy-done, s32[1,128]{1,0:T(1,128)S(1)} %bitcast.1, bf16[256,256]{1,0:T(8,128)(2,1)S(1)} %copy-done.1, ...), custom_call_target="tpu_custom_call" | custom-call | tf_op jit(solution)/shard_map/gather_messages/pallas_call | solution.py:203
  46.3 0.0 copy-start.5
  46.3 0.7 copy-done.5
  46.9 0.0 copy-start.6
  46.9 0.7 copy-done.6
  47.6 11.6 %edge_sums.1 = (bf16[4,16,2,32,128]{4,3,2,1,0:T(8,128)(2,1)S(1)}, s32[16]{0:T(128)S(1)}, s32[32]{0:T(128)S(1)}, s32[16]{0:T(128)S(1)}) custom-call(s32[256]{0:T(256)S(1)} %copy-done.5, s32[256]{0:T(256)S(1)} %copy-done.6, s32[1]{0:T(128)S(6)} %copy.14.live_ref, s32[16,8,128]{2,1,0:T(8,128)S(1)} %get-tuple-element.10.ids_ref, ...), custom_call_target="tpu_custom_call" | custom-call | tf_op jit(solution)/shard_map/edge_sums/pallas_call | solution.py:312
  59.2 0.0 copy-done.4
  59.3 122.4 %merge_mirrors.1 = (bf16[128,256]{1,0:T(8,128)(2,1)S(1)}, bf16[1,16,128,256]{3,2,1,0:T(8,128)(2,1)S(1)}) custom-call(bf16[4,16,2,32,128]{4,3,2,1,0:T(8,128)(2,1)S(1)} %get-tuple-element.14.part_ref, s32[16]{0:T(128)S(1)} %get-tuple-element.15.prev_ref, s32[32]{0:T(128)S(1)} %get-tuple-element.16.last_ref, s32[16]{0:T(128)S(1)} %get-tuple-element.17.tid_ref, ...), custom_call_target="tpu_custom_call" | custom-call | tf_op jit(solution)/shard_map/merge_mirrors/pallas_call | solution.py:623
  181.6 0.6 copy.15
  182.3 1.0 copy.16
Async XLA Ops:
  1.3 0.8 copy-start
  2.1 0.9 copy-start.1
  3.0 0.9 copy-start.2
  3.9 0.9 copy-start.3
  4.8 0.7 copy-start.7
  5.5 0.7 copy-start.8
  6.1 53.1 %copy-start.4 = (bf16[256,256]{1,0:T(8,128)(2,1)S(1)}, bf16[256,256]{1,0:T(8,128)(2,1)}, u32[]{:S(2)}) copy-start(bf16[256,256]{1,0:T(8,128)(2,1)} %w_ref.3) | copy-start | bytes 393220
  46.3 0.7 copy-start.5
  46.9 0.7 copy-start.6

commit v2 on v1

v2 whole, which is shorter than its diff:
```python
import functools

import jax
import jax.numpy as jnp
from jax import lax
from jax.experimental import pallas as pl
from jax.experimental.pallas import tpu as pltpu
from jax.sharding import PartitionSpec as P

MESH = pl.DeviceIdType.MESH
NX, NY = 4, 8
NE = NX * NY
NG = 16
TILE = 128
D = 256
H = 128
B = 256
CHUNKS = 4
R = TILE // CHUNKS
VMEM_LIMIT = 40 * 1024 * 1024
LAG = 1
F32 = jnp.float32
BF16 = jnp.bfloat16
NT = (((1,), (1,)), ((), ()))


def here():
    e = lax.axis_index("edge")
    return lax.div(e, NY), lax.rem(e, NY)


def wrap_x(x):
    return lax.rem(x + 2 * NX, NX)


def wrap_y(y):
    return lax.rem(y + 2 * NY, NY)


def node(x, y):
    return {"edge": wrap_x(x) * NY + wrap_y(y)}


def plane_peers():
    x, y = here()
    return [node(x + j, y) for j in (1, 2, 3)] + [node(x, y + j) for j in (1, -1, 2, -2)]


def greet():
    barrier = pltpu.get_barrier_semaphore()
    peers = plane_peers()
    for peer in peers:
        pl.semaphore_signal(barrier, inc=1, device_id=peer, device_id_type=MESH)
    me = lax.axis_index("grp")

    def signal(i, carry):
        pl.semaphore_signal(
            barrier, inc=1, device_id={"grp": lax.rem(me + i, NG)}, device_id_type=MESH
        )
        return carry

    lax.fori_loop(1, NG, signal, 0)
    pl.semaphore_wait(barrier, len(peers) + NG - 1)


def gather_copies(fa, fb, send, recv):
    x, y = here()
    rows = fa.shape[1]

    def along_x(ref):
        return [(ref, node(x + j, y)) for j in (1, 2, 3)]

    def near_y(ref):
        return [(ref, node(x, y + j)) for j in (1, -1, 2, -2)]

    def group_a(yy):
        return wrap_y(yy) * NX

    def group_b(yy):
        return x * NY + wrap_y(yy)

    def half_b(yy, d):
        return fb.at[pl.ds(group_b(yy), 1), pl.ds(d * (rows // 2), rows // 2)]

    plan = [
        [
            along_x(fa.at[pl.ds(y * NX + x, 1)]),
            near_y(fa.at[pl.ds(y * NX, NX)]),
            [
                (fa.at[pl.ds(group_a(y - 2), NX)], node(x, y + 1)),
                (fa.at[pl.ds(group_a(y + 2), NX)], node(x, y - 1)),
                (fa.at[pl.ds(group_a(y - 2) + NX // 2, NX // 2)], node(x, y + 2)),
                (fa.at[pl.ds(group_a(y + 2), NX // 2)], node(x, y - 2)),
            ],
        ],
        [
            near_y(fb.at[pl.ds(group_b(y), 1)]),
            [
                (fb.at[pl.ds(group_b(y - 2), 1)], node(x, y + 1)),
                (fb.at[pl.ds(group_b(y + 2), 1)], node(x, y - 1)),
                (half_b(y - 2, 1), node(x, y + 2)),
                (half_b(y + 2, 0), node(x, y - 2)),
            ],
            along_x(fb.at[pl.ds(x * NY, NY)]),
        ],
    ]
    out = []
    for color in range(2):
        n = 0
        steps = []
        for step in plan[color]:
            copies = []
            for ref, to in step:
                copies.append(
                    pltpu.make_async_remote_copy(
                        src_ref=ref,
                        dst_ref=ref,
                        send_sem=send.at[color, n],
                        recv_sem=recv.at[color, n],
                        device_id=to,
                        device_id_type=MESH,
                    )
                )
                n += 1
            steps.append(copies)
        out.append(steps)
    return out


def gather_step(copies, color, stage):
    if stage > 0:
        for c in copies[color][stage - 1]:
            c.wait_recv()
    if stage < 3:
        for c in copies[color][stage]:
            c.start()


def gather_stage(copies, stage):
    for color in (1, 0):
        gather_step(copies, color, stage)


def gather_finish(copies):
    for color in range(2):
        for row in copies[color]:
            for c in row:
                c.wait_send()


SLOTS = 384


def block_order(group, tile, live):
    spread = jnp.broadcast_to(group, (TILE, B))
    slot_id = lax.broadcasted_iota(jnp.int32, (TILE, B), 1)
    mine = (lax.broadcasted_iota(jnp.int32, (TILE, B), 0) == spread) & (slot_id < live)
    hot = mine.astype(F32)
    before = lax.broadcasted_iota(jnp.int32, (B, B), 0) < lax.broadcasted_iota(
        jnp.int32, (B, B), 1
    )
    rank = jnp.dot(hot.astype(BF16), before.astype(F32).astype(BF16), preferred_element_type=F32)
    count = jnp.sum(hot, axis=1, keepdims=True).astype(jnp.int32)
    pairs = (count + 1) >> 1
    lower = lax.broadcasted_iota(jnp.int32, (TILE, TILE), 1) < lax.broadcasted_iota(
        jnp.int32, (TILE, TILE), 0
    )
    pairs_f = jnp.broadcast_to(pairs.astype(F32), (TILE, TILE))
    first = jnp.dot(
        lower.astype(F32).astype(BF16), pairs_f.astype(BF16), preferred_element_type=F32
    )
    place = 2.0 * first[:, 0:1] + rank + 1.0
    place = jnp.sum(hot * place, axis=0, keepdims=True).astype(jnp.int32) - 1
    hit = lax.broadcasted_iota(jnp.int32, (SLOTS, B), 0) == place
    row = lax.broadcasted_iota(jnp.int32, (8, B), 0)
    lane = lax.broadcasted_iota(jnp.int32, (8, B), 1)
    facts = jnp.where(row == 0, lane - B, jnp.where(row == 1, tile, group))
    found = lax.dot_general(
        facts.astype(F32).astype(BF16),
        hit.astype(F32).astype(BF16),
        NT,
        preferred_element_type=F32,
    ).astype(jnp.int32)
    row = lax.broadcasted_iota(jnp.int32, (8, SLOTS), 0)
    total = jnp.sum(pairs, axis=0, keepdims=True)
    return jnp.where(row == 0, found + B, jnp.where(row == 3, total, found))


def gather_kernel(
    g_any, deg_any, w_any, es_any, ed_any, mt_any, sg_any, dt_any, live_any,
    ma_ref, mb_ref, counts_ref, ids_ref, order_ref,
    g_ref, deg_ref, w_ref, es_ref, ed_ref, mt_ref, sg_ref, dt_ref, live_ref,
    in_sem, send, recv, id_send, id_recv,
):
    x, y = here()
    me = lax.axis_index("grp")
    pairs = (
        (g_any, g_ref), (w_any, w_ref), (deg_any, deg_ref), (mt_any, mt_ref), (sg_any, sg_ref),
        (dt_any, dt_ref), (live_any, live_ref), (es_any, es_ref), (ed_any, ed_ref),
    )
    loads = [
        pltpu.make_async_copy(src, dst, in_sem.at[i]) for i, (src, dst) in enumerate(pairs)
    ]
    for c in loads:
        c.start()
    for c in loads[:4]:
        c.wait()
    ids_ref[pl.ds(me, 1)] = jnp.zeros((1, 8, 128), jnp.int32)
    ids_ref[pl.ds(me, 1), 0:1, 0:NG] = mt_ref[...].reshape(1, 1, NG)
    neigh = lax.dot_general(g_ref[...], w_ref[...], NT, preferred_element_type=F32)
    deg = jnp.broadcast_to(deg_ref[...].astype(F32), (TILE, TILE)).T
    ma_ref[pl.ds(y * NX + x, 1)] = (neigh[:, :H] / deg).astype(BF16)[None]
    mb_ref[pl.ds(x * NY + y, 1)] = (neigh[:, H:] / deg).astype(BF16)[None]
    greet()

    copies = gather_copies(ma_ref, mb_ref, send, recv)
    rows_id = lax.broadcasted_iota(jnp.int32, (TILE, TILE), 0)

    def id_copy(i):
        peer = lax.rem(me + i, NG)
        return pltpu.make_async_remote_copy(
            src_ref=ids_ref.at[pl.ds(me, 1)],
            dst_ref=ids_ref.at[pl.ds(me, 1)],
            send_sem=id_send.at[i],
            recv_sem=id_recv.at[i],
            device_id={"grp": peer},
            device_id_type=MESH,
        )

    def one(b):
        src = (rows_id == es_ref[pl.ds(b, 1), :]).astype(F32).astype(BF16)
        dst = (rows_id == ed_ref[pl.ds(b, 1), :]).astype(F32).astype(BF16)
        counts_ref[pl.ds(b, 1)] = lax.dot_general(
            src, dst, NT, preferred_element_type=F32
        ).astype(BF16)[None]

    per_part = B // 8

    def build(first_part, parts):
        def body(i, carry):
            b = first_part * per_part + i * 8
            for j in range(8):
                one(b + j)
            return carry

        lax.fori_loop(0, parts * per_part // 8, body, 0)

    gather_stage(copies, 0)

    def start_id(i, carry):
        id_copy(i).start()
        return carry

    lax.fori_loop(1, NG, start_id, 0)
    for c in loads[4:]:
        c.wait()
    order_ref[...] = block_order(sg_ref[...], dt_ref[...], live_ref[...])
    counts_ref[B] = jnp.zeros((TILE, TILE), BF16)
    gather_step(copies, 0, 1)
    gather_step(copies, 1, 1)
    build(0, 1)
    gather_step(copies, 1, 2)
    build(1, 3)
    gather_step(copies, 0, 2)
    build(4, 4)
    gather_stage(copies, 3)

    def end_id(i, carry):
        id_copy(i).wait()
        return carry

    lax.fori_loop(1, NG, end_id, 0)
    gather_finish(copies)


def gather(grad_out, deg, w_neigh, edge_src, edge_dst, mirror_tiles, group, tile, live):
    vmem = pl.BlockSpec(memory_space=pltpu.VMEM)
    ins = (grad_out, deg, w_neigh, edge_src, edge_dst, mirror_tiles, group, tile, live)
    return pl.pallas_call(
        gather_kernel,
        out_shape=(
            jax.ShapeDtypeStruct((NE, TILE, H), BF16),
            jax.ShapeDtypeStruct((NE, TILE, H), BF16),
            jax.ShapeDtypeStruct((B + 1, TILE, TILE), BF16),
            jax.ShapeDtypeStruct((NG, 8, 128), jnp.int32),
            jax.ShapeDtypeStruct((8, SLOTS), jnp.int32),
        ),
        in_specs=[pl.BlockSpec(memory_space=pltpu.HBM)] * len(ins),
        out_specs=(vmem,) * 5,
        scratch_shapes=[pltpu.VMEM(v.shape, v.dtype) for v in ins]
        + [
            pltpu.SemaphoreType.DMA((len(ins),)),
            pltpu.SemaphoreType.DMA((2, 11)),
            pltpu.SemaphoreType.DMA((2, 11)),
            pltpu.SemaphoreType.DMA((NG,)),
            pltpu.SemaphoreType.DMA((NG,)),
        ],
        compiler_params=pltpu.CompilerParams(
            collective_id=0, has_side_effects=True, vmem_limit_bytes=VMEM_LIMIT
        ),
        name="gather_messages",
    )(*ins)


UNROLL = 4


def sum_kernel(
    order_ref, ids_ref, counts_ref, ma_ref, mb_ref,
    part_ref, prev_ref, last_ref, tid_ref,
    sums,
):
    me = lax.axis_index("grp")

    def clear(t, carry):
        last_ref[t] = NG
        return carry

    lax.fori_loop(0, NE, clear, 0)

    def link(g, carry):
        t = ids_ref[g, 0, me]
        tid_ref[g] = t
        prev_ref[g] = last_ref[t]
        last_ref[t] = g
        return carry

    lax.fori_loop(0, NG, link, 0)
    sums[...] = jnp.zeros_like(sums)

    def tile_of(t):
        ia = lax.rem(t, NY) * NX + lax.div(t, NY)
        return jnp.concatenate([ma_ref[ia], mb_ref[t]], axis=1)

    def turn(i, carry):
        for j in range(UNROLL):
            p = 2 * (i * UNROLL + j)
            lhs = jnp.concatenate(
                [counts_ref[order_ref[0, p]], counts_ref[order_ref[0, p + 1]]], axis=1
            )
            rhs = jnp.concatenate(
                [tile_of(order_ref[1, p]), tile_of(order_ref[1, p + 1])], axis=0
            )
            s = order_ref[2, p]
            sums[s] = sums[s] + jnp.dot(lhs, rhs, preferred_element_type=F32)
        return carry

    lax.fori_loop(0, lax.div(order_ref[3, 0] + UNROLL - 1, UNROLL), turn, 0)

    def write(s, carry):
        for c in range(CHUNKS):
            for h in range(2):
                part_ref[c, s, h] = sums[s, c * R : (c + 1) * R, h * H : (h + 1) * H].astype(BF16)
        return carry

    lax.fori_loop(0, NG, write, 0)


def edge_sums(order, ids, counts, ma, mb):
    smem = pl.BlockSpec(memory_space=pltpu.SMEM)
    vmem = pl.BlockSpec(memory_space=pltpu.VMEM)
    return pl.pallas_call(
        sum_kernel,
        out_shape=(
            jax.ShapeDtypeStruct((CHUNKS, NG, 2, R, H), BF16),
            jax.ShapeDtypeStruct((NG,), jnp.int32),
            jax.ShapeDtypeStruct((NE,), jnp.int32),
            jax.ShapeDtypeStruct((NG,), jnp.int32),
        ),
        in_specs=[smem, smem, vmem, vmem, vmem],
        out_specs=(vmem, smem, smem, smem),
        scratch_shapes=[pltpu.VMEM((NG, TILE, D), F32)],
        compiler_params=pltpu.CompilerParams(vmem_limit_bytes=VMEM_LIMIT),
        name="edge_sums",
    )(order, ids, counts, ma, mb)


NAMES = (
    "relay", "sums", "ua", "ub", "fa", "fb", "picked",
    "sfara", "sneara", "shalfa", "smida", "sxa", "sfarb", "snearb", "shalfb", "smidb", "sxb",
    "rfara", "rneara", "rhalfa", "rmida", "rxa", "rfarb", "rnearb", "rhalfb", "rmidb", "rxb",
)
Z_ORDER = (8, 9, 7, 6, 10, 5, 11, 4, 12, 3, 13, 2, 14, 1, 15)


def merge_kernel(
    part_ref, prev_ref, last_ref, tid_ref, g_any, w_any,
    gf_ref, mg_ref,
    g_ref, w_ref, in_sem,
    self_term, own_sem, z_send, z_recv, r_send, r_recv, f_send, f_recv, b_send, b_recv,
    *bufs,
):
    x, y = here()
    me = lax.axis_index("grp")
    chunks = [dict(zip(NAMES, bufs[c * len(NAMES) : (c + 1) * len(NAMES)])) for c in range(CHUNKS)]
    loads = [
        pltpu.make_async_copy(g_any, g_ref, in_sem.at[0]),
        pltpu.make_async_copy(w_any, w_ref, in_sem.at[1]),
    ]
    for c in loads:
        c.start()

    greet()

    def z_copy(c, i):
        peer = lax.rem(me + i, NG)
        return pltpu.make_async_remote_copy(
            src_ref=part_ref.at[c, peer],
            dst_ref=chunks[c]["relay"].at[me],
            send_sem=z_send.at[c, i],
            recv_sem=z_recv.at[c, i],
            device_id={"grp": peer},
            device_id_type=MESH,
        )

    def own_copy(c):
        return pltpu.make_async_copy(
            part_ref.at[c, me], chunks[c]["relay"].at[me], own_sem.at[c]
        )

    for c in range(CHUNKS):
        own_copy(c).start()
        for i in Z_ORDER:
            z_copy(c, i).start()

    for c in loads:
        c.wait()
    self_term[...] = lax.dot_general(g_ref[...], w_ref[...], NT, preferred_element_type=F32)

    y_hop = (1, -1, 1, -1, 2, -2, 2, -2)

    def ring_copy(c, color, n):
        buf = chunks[c]
        kind = ("far", "near", "half", "mid")[n // 2] if n < 8 else "x"
        d = n % 2 if n < 8 else n - 8
        to = node(x, y + y_hop[n]) if n < 8 else node(x + d + 1, y)
        name = kind + "ab"[color]
        return pltpu.make_async_remote_copy(
            src_ref=buf["s" + name].at[d],
            dst_ref=buf["r" + name].at[d],
            send_sem=r_send.at[c, color, n],
            recv_sem=r_recv.at[c, color, n],
            device_id=to,
            device_id_type=MESH,
        )

    def start(c, color, which):
        for n in which:
            ring_copy(c, color, n).start()

    def arrived(c, color, which):
        for n in which:
            ring_copy(c, color, n).wait_recv()

    first, second, cross = (0, 1, 2, 3, 4, 5), (6, 7), (8, 9, 10)

    def tile_sum(c, color, xx, yy):
        return chunks[c]["sums"][last_ref[xx * NY + yy], color]

    def relay_stage(c):
        buf = chunks[c]
        own_copy(c).wait()

        def arrive(i, carry):
            z_copy(c, i).wait_recv()
            return carry

        lax.fori_loop(1, NG, arrive, 0)
        buf["sums"][NG] = jnp.zeros((2, R, H), F32)
        for g in range(NG):
            buf["sums"][g] = buf["relay"][g].astype(F32) + buf["sums"][prev_ref[g]]

    half_rows = R // 2

    def reduce_a(c, k):
        buf = chunks[c]
        if k == 0:
            for d in range(2):
                sign = 1 - 2 * d
                for xx in range(NX):
                    buf["sfara"][d, xx] = tile_sum(c, 0, xx, wrap_y(y + 3 * sign)).astype(BF16)
                    buf["sneara"][d, xx] = tile_sum(c, 0, xx, wrap_y(y + sign)).astype(BF16)
                for j in range(2):
                    buf["shalfa"][d, j] = tile_sum(c, 0, 2 * d + j, wrap_y(y + 4)).astype(BF16)
            start(c, 0, first)
        elif k == 1:
            arrived(c, 0, first)
            for d in range(2):
                yy = wrap_y(y + 2 * (1 - 2 * d))
                for xx in range(NX):
                    v = tile_sum(c, 0, xx, yy) + buf["rfara"][d, xx].astype(F32)
                    if xx // 2 == d:
                        v = v + buf["rhalfa"][d, xx % 2].astype(F32)
                    buf["smida"][d, xx] = v.astype(BF16)
            start(c, 0, second)
        elif k == 2:
            arrived(c, 0, second)
            for xx in range(NX):
                v = tile_sum(c, 0, xx, y)
                for d in range(2):
                    v = v + buf["rneara"][d, xx].astype(F32) + buf["rmida"][d, xx].astype(F32)
                buf["ua"][xx] = v
            for j in range(3):
                buf["sxa"][j] = buf["ua"][wrap_x(x + j + 1)].astype(BF16)
            start(c, 0, cross)
        else:
            arrived(c, 0, cross)
            v = buf["ua"][x]
            for j in range(3):
                v = v + buf["rxa"][j].astype(F32)
            return v

    def reduce_b(c, k):
        buf = chunks[c]
        if k == 0:
            for j in range(3):
                xx = wrap_x(x + j + 1)
                for yy in range(NY):
                    buf["sxb"][j, yy] = tile_sum(c, 1, xx, yy).astype(BF16)
            start(c, 1, cross)
        elif k == 1:
            arrived(c, 1, cross)
            for yy in range(NY):
                v = tile_sum(c, 1, x, yy)
                for j in range(3):
                    v = v + buf["rxb"][j, yy].astype(F32)
                buf["ub"][yy] = v
            for d in range(2):
                sign = 1 - 2 * d
                buf["sfarb"][d] = buf["ub"][wrap_y(y + 3 * sign)].astype(BF16)
                buf["snearb"][d] = buf["ub"][wrap_y(y + sign)].astype(BF16)
                half = pl.ds(d * half_rows, half_rows)
                buf["shalfb"][d] = buf["ub"][wrap_y(y + 4), half].astype(BF16)
            start(c, 1, first)
        elif k == 2:
            arrived(c, 1, first)
            for d in range(2):
                v = buf["ub"][wrap_y(y + 2 * (1 - 2 * d))] + buf["rfarb"][d].astype(F32)
                parts = [v[:half_rows], v[half_rows:]]
                parts[d] = parts[d] + buf["rhalfb"][d].astype(F32)
                for j in range(2):
                    buf["smidb"][d, j * half_rows : (j + 1) * half_rows] = parts[j].astype(BF16)
            start(c, 1, second)
        else:
            arrived(c, 1, second)
            v = buf["ub"][y]
            for d in range(2):
                v = v + buf["rnearb"][d].astype(F32) + buf["rmidb"][d].astype(F32)
            return v

    gathers = [
        gather_copies(chunks[c]["fa"], chunks[c]["fb"], f_send.at[c], f_recv.at[c])
        for c in range(CHUNKS)
    ]

    def back_copy(c, i):
        peer = lax.rem(me + i, NG)
        return pltpu.make_async_remote_copy(
            src_ref=chunks[c]["picked"].at[peer],
            dst_ref=mg_ref.at[0, me, pl.ds(c * R, R)],
            send_sem=b_send.at[c, i],
            recv_sem=b_recv.at[c, i],
            device_id={"grp": peer},
            device_id_type=MESH,
        )

    def back_own(c):
        return pltpu.make_async_copy(
            chunks[c]["picked"].at[me], mg_ref.at[0, me, pl.ds(c * R, R)], own_sem.at[CHUNKS + c]
        )

    def finish_tile(c):
        buf = chunks[c]
        own_a = reduce_a(c, 3)
        own_b = reduce_b(c, 3)
        rows = pl.ds(c * R, R)
        out_a = (self_term[rows, 0:H] + own_a).astype(BF16)
        out_b = (self_term[rows, H:D] + own_b).astype(BF16)
        gf_ref[rows, 0:H] = out_a
        gf_ref[rows, H:D] = out_b
        buf["fa"][pl.ds(y * NX + x, 1)] = out_a[None]
        buf["fb"][pl.ds(x * NY + y, 1)] = out_b[None]
        gather_stage(gathers[c], 0)

    def send_back(c):
        buf = chunks[c]
        gather_stage(gathers[c], 3)
        for g in range(NG):
            t = tid_ref[g]
            ia = lax.rem(t, NY) * NX + lax.div(t, NY)
            buf["picked"][g, :, 0:H] = buf["fa"][ia]
            buf["picked"][g, :, H:D] = buf["fb"][t]
        back_own(c).start()
        for i in Z_ORDER:
            back_copy(c, i).start()

    stages = []
    for k in range(3):
        def reduce_step(c, k=k):
            if k == 0:
                relay_stage(c)
            reduce_a(c, k)
            reduce_b(c, k)
        stages.append(reduce_step)
    stages.append(finish_tile)
    for k in range(1, 3):
        stages.append(lambda c, k=k: gather_stage(gathers[c], k))
    stages.append(send_back)

    lag = LAG
    for tick in range(len(stages) + lag * (CHUNKS - 1)):
        for c in range(CHUNKS):
            k = tick - lag * c
            if 0 <= k < len(stages):
                stages[k](c)

    for c in range(CHUNKS):
        back_own(c).wait()

        def end(i, carry, c=c):
            z_copy(c, i).wait_send()
            back_copy(c, i).wait()
            return carry

        lax.fori_loop(1, NG, end, 0)
        for color in range(2):
            for n in range(11):
                ring_copy(c, color, n).wait_send()
        gather_finish(gathers[c])


def merge(part, prev, last, tid, grad_out, w_self):
    smem = pl.BlockSpec(memory_space=pltpu.SMEM)
    vmem = pl.BlockSpec(memory_space=pltpu.VMEM)
    hbm = pl.BlockSpec(memory_space=pl.ANY)
    kept = pl.BlockSpec(memory_space=pltpu.HBM)
    half = R // 2
    shapes = dict(
        relay=((NG, 2, R, H), BF16),
        sums=((NG + 1, 2, R, H), F32),
        ua=((NX, R, H), F32),
        ub=((NY, R, H), F32),
        fa=((NE, R, H), BF16),
        fb=((NE, R, H), BF16),
        picked=((NG, R, D), BF16),
    )
    for side in "sr":
        shapes[side + "fara"] = ((2, NX, R, H), BF16)
        shapes[side + "neara"] = ((2, NX, R, H), BF16)
        shapes[side + "halfa"] = ((2, NX // 2, R, H), BF16)
        shapes[side + "mida"] = ((2, NX, R, H), BF16)
        shapes[side + "xa"] = ((3, R, H), BF16)
        shapes[side + "farb"] = ((2, R, H), BF16)
        shapes[side + "nearb"] = ((2, R, H), BF16)
        shapes[side + "halfb"] = ((2, half, H), BF16)
        shapes[side + "midb"] = ((2, R, H), BF16)
        shapes[side + "xb"] = ((3, NY, R, H), BF16)
    per_chunk = [pltpu.VMEM(*shapes[name]) for name in NAMES]
    dma = pltpu.SemaphoreType.DMA
    return pl.pallas_call(
        merge_kernel,
        out_shape=(
            jax.ShapeDtypeStruct((TILE, D), BF16),
            jax.ShapeDtypeStruct((1, NG, TILE, D), BF16),
        ),
        in_specs=[hbm, smem, smem, smem, kept, kept],
        out_specs=(vmem, hbm),
        scratch_shapes=[
            pltpu.VMEM((TILE, D), BF16),
            pltpu.VMEM((D, D), BF16),
            dma((2,)),
            pltpu.VMEM((TILE, D), F32),
            dma((2 * CHUNKS,)),
            dma((CHUNKS, NG)),
            dma((CHUNKS, NG)),
            dma((CHUNKS, 2, 11)),
            dma((CHUNKS, 2, 11)),
            dma((CHUNKS, 2, 11)),
            dma((CHUNKS, 2, 11)),
            dma((CHUNKS, NG)),
            dma((CHUNKS, NG)),
        ]
        + per_chunk * CHUNKS,
        compiler_params=pltpu.CompilerParams(
            collective_id=1, has_side_effects=True, vmem_limit_bytes=VMEM_LIMIT
        ),
        name="merge_mirrors",
    )(part, prev, last, tid, grad_out, w_self)


def per_device(
    grad_out,
    in_degree,
    w_self,
    w_neigh,
    block_dst_tile,
    block_src_group,
    edge_dst,
    edge_src,
    block_count,
    mirror_tiles,
):
    ma, mb, counts, ids, order = gather(
        grad_out,
        in_degree.reshape(1, -1),
        w_neigh,
        edge_src,
        edge_dst,
        mirror_tiles,
        block_src_group.reshape(1, -1),
        block_dst_tile.reshape(1, -1),
        block_count.reshape(1, 1),
    )
    part, prev, last, tid = edge_sums(order, ids, counts, ma, mb)
    return merge(part, prev, last, tid, grad_out, w_self)


def solution(mesh):
    placed = (
        P(("grp", "edge"), None),
        P(("grp", "edge")),
        P(),
        P(),
        P(("grp", "edge")),
        P(("grp", "edge")),
        P(("grp", "edge"), None),
        P(("grp", "edge"), None),
        P(("grp", "edge")),
        P(("grp", "edge"), None),
    )
    return jax.shard_map(
        per_device,
        mesh=mesh,
        in_specs=placed,
        out_specs=(P(("grp", "edge"), None), P(("grp", "edge"), None, None, None)),
        check_vma=False,
    )
```

time: 184 us -> 141 us (0.77)
  Pallas kernels: 174 us -> 132 us
    pallas_call x1, Pallas kernels: 122 us -> 81.9 us  [merge(): pl.pallas_call(merge_kernel, out_shape=(jax.ShapeDtypeStruct((TILE, D), B...]
    pallas_call x1, Pallas kernels: 11.6 us -> 8.6 us  [edge_sums(): pl.pallas_call(sum_kernel, out_shape=(jax.ShapeDtypeStruct((CHUNKS, NG, 2...]
where the time goes in v2:
time: 141 us
  Pallas kernels  132 us (94%)
  local copies, waits for them, and re-layouts  7.82 us (6%)
    pallas_call x1, Pallas kernels, merge(): pl.pallas_call(merge_kernel, out_shape=(jax.ShapeDtypeStruct((TILE, D), B...  81.9 us
    pallas_call x1, Pallas kernels, gather(): pl.pallas_call(gather_kernel, out_shape=(jax.ShapeDtypeStruct((NE, TILE,...  41.2 us
    pallas_call x1, Pallas kernels, edge_sums(): pl.pallas_call(sum_kernel, out_shape=(jax.ShapeDtypeStruct((CHUNKS, NG, 2...  8.6 us
    unnamed x20, local copies, waits for them, and re-layouts  7.82 us

profile of v2, /device:TPU:1, one launch (start us, length us, event | category | flops | bytes accessed | tf_op | source)
XLA Modules:
  0.0 140.9 jit_solution(10256034158547886521)
XLA Ops:
  1.3 0.0 copy-start
  1.3 0.8 copy-done
  2.1 0.0 copy-start.1
  2.1 0.9 copy-done.1
  3.0 0.0 copy-start.2
  3.0 0.9 copy-done.2
  3.9 0.0 copy-start.3
  3.9 0.9 copy-done.3
  4.8 0.0 copy-start.5
  4.8 0.7 copy-done.5
  5.5 0.0 copy-start.6
  5.5 0.7 copy-done.6
  6.2 0.0 copy-start.7
  6.2 0.7 copy-done.7
  6.8 0.0 copy-start.8
  6.9 0.7 copy-done.8
  7.5 0.0 copy-start.4
  7.5 41.2 %gather_messages.1 = (bf16[32,128,128]{2,1,0:T(8,128)(2,1)S(1)}, bf16[32,128,128]{2,1,0:T(8,128)(2,1)S(1)}, bf16[257,128,128]{2,1,0:T(8,128)(2,1)S(1)}, s32[16,8,128]{2,1,0:T(8,128)S(1)}, s32[8,384]{1,0:T(8,128)S(1)}) custom-call(bf16[128,256]{1,0:T(8,128)(2,1)S(1)} %copy-done, s32[1,128]{1,0:T(1,128)S(1)} %bitcast.7, bf16[256,256]{1,0:T(8,128)(2,1)S(1)} %copy-done.1, ...), custom_call_target="tpu_custom_call" | custom-call | tf_op jit(solution)/shard_map/gather_messages/pallas_call | solution.py:279
  48.8 8.6 %edge_sums.1 = (bf16[4,16,2,32,128]{4,3,2,1,0:T(8,128)(2,1)S(1)}, s32[16]{0:T(128)S(1)}, s32[32]{0:T(128)S(1)}, s32[16]{0:T(128)S(1)}) custom-call(s32[8,384]{1,0:T(8,128)S(1)} %get-tuple-element.11.order_ref, s32[16,8,128]{2,1,0:T(8,128)S(1)} %get-tuple-element.12.ids_ref, bf16[257,128,128]{2,1,0:T(8,128)(2,1)S(1)} %get-tuple-element.13.counts_ref, ...), custom_call_target="tpu_custom_call" | custom-call | tf_op jit(solution)/shard_map/edge_sums/pallas_call | solution.py:362
  57.4 0.0 copy-done.4
  57.4 81.9 %merge_mirrors.1 = (bf16[128,256]{1,0:T(8,128)(2,1)S(1)}, bf16[1,16,128,256]{3,2,1,0:T(8,128)(2,1)S(1)}) custom-call(bf16[4,16,2,32,128]{4,3,2,1,0:T(8,128)(2,1)S(1)} %get-tuple-element.16.part_ref, s32[16]{0:T(128)S(1)} %get-tuple-element.17.prev_ref, s32[32]{0:T(128)S(1)} %get-tuple-element.18.last_ref, s32[16]{0:T(128)S(1)} %get-tuple-element.19.tid_ref, ...), custom_call_target="tpu_custom_call" | custom-call | tf_op jit(solution)/shard_map/merge_mirrors/pallas_call | solution.py:660
  139.3 0.6 copy.15
  139.9 1.0 copy.16
Async XLA Ops:
  1.3 0.8 copy-start
  2.1 0.9 copy-start.1
  3.0 0.9 copy-start.2
  3.9 0.9 copy-start.3
  4.8 0.7 copy-start.5
  5.5 0.7 copy-start.6
  6.2 0.7 copy-start.7
  6.8 0.7 copy-start.8
  7.5 49.9 %copy-start.4 = (bf16[256,256]{1,0:T(8,128)(2,1)S(1)}, bf16[256,256]{1,0:T(8,128)(2,1)}, u32[]{:S(2)}) copy-start(bf16[256,256]{1,0:T(8,128)(2,1)} %w_any.3) | copy-start | bytes 393220

commit v3 on v2

--- a/solution.py
+++ b/solution.py
@@ -299,7 +299,7 @@
             collective_id=0, has_side_effects=True, vmem_limit_bytes=VMEM_LIMIT
         ),
         name="gather_messages",
-    )(*ins)
+    )(*[pltpu.with_memory_space_constraint(v, pltpu.HBM) for v in ins[:-1]], live)
 
 
 UNROLL = 4

time: 141 us -> 135 us (0.957)
  local copies, waits for them, and re-layouts: 7.82 us -> 1.61 us
    unnamed x20 -> x6, local copies, waits for them, and re-layouts: 7.82 us -> 1.61 us
    pallas_call x1, Pallas kernels: 8.6 us -> 5.7 us  [edge_sums(): pl.pallas_call(sum_kernel, out_shape=(jax.ShapeDtypeStruct((CHUNKS, NG, 2...]
    pallas_call x1, Pallas kernels: 81.9 us -> 84.5 us  [merge(): pl.pallas_call(merge_kernel, out_shape=(jax.ShapeDtypeStruct((TILE, D), B...]
where the time goes in v3:
time: 135 us
  Pallas kernels  132 us (98%)
  local copies, waits for them, and re-layouts  1.61 us (1%)
  between operations  1.37 us (1%)
    pallas_call x1, Pallas kernels, merge(): pl.pallas_call(merge_kernel, out_shape=(jax.ShapeDtypeStruct((TILE, D), B...  84.5 us
    pallas_call x1, Pallas kernels, gather(): pl.pallas_call(gather_kernel, out_shape=(jax.ShapeDtypeStruct((NE, TILE,...  41.5 us
    pallas_call x1, Pallas kernels, edge_sums(): pl.pallas_call(sum_kernel, out_shape=(jax.ShapeDtypeStruct((CHUNKS, NG, 2...  5.7 us

profile of v3, /device:TPU:1, one launch (start us, length us, event | category | flops | bytes accessed | tf_op | source)
XLA Modules:
  0.0 134.6 jit_solution(10340040464494982357)
XLA Ops:
  0.6 0.0 copy-start
  0.6 0.0 copy-start.1
  1.3 41.5 %gather_messages.1 = (bf16[32,128,128]{2,1,0:T(8,128)(2,1)S(1)}, bf16[32,128,128]{2,1,0:T(8,128)(2,1)S(1)}, bf16[257,128,128]{2,1,0:T(8,128)(2,1)S(1)}, s32[16,8,128]{2,1,0:T(8,128)S(1)}, s32[8,384]{1,0:T(8,128)S(1)}) custom-call(bf16[128,256]{1,0:T(8,128)(2,1)} %g_any.3, s32[1,128]{1,0:T(1,128)} %bitcast.7, bf16[256,256]{1,0:T(8,128)(2,1)} %w_any.2, ...), custom_call_target="tpu_custom_call" | custom-call | tf_op jit(solution)/shard_map/gather_messages/pallas_call | solution.py:279
  42.8 5.7 %edge_sums.1 = (bf16[4,16,2,32,128]{4,3,2,1,0:T(8,128)(2,1)S(1)}, s32[16]{0:T(128)S(1)}, s32[32]{0:T(128)S(1)}, s32[16]{0:T(128)S(1)}) custom-call(s32[8,384]{1,0:T(8,128)S(1)} %get-tuple-element.11.order_ref, s32[16,8,128]{2,1,0:T(8,128)S(1)} %get-tuple-element.12.ids_ref, bf16[257,128,128]{2,1,0:T(8,128)(2,1)S(1)} %get-tuple-element.13.counts_ref, ...), custom_call_target="tpu_custom_call" | custom-call | tf_op jit(solution)/shard_map/edge_sums/pallas_call | solution.py:362
  48.5 0.0 copy-done
  48.5 0.0 copy-done.1
  48.5 84.5 %merge_mirrors.1 = (bf16[128,256]{1,0:T(8,128)(2,1)S(1)}, bf16[1,16,128,256]{3,2,1,0:T(8,128)(2,1)S(1)}) custom-call(bf16[4,16,2,32,128]{4,3,2,1,0:T(8,128)(2,1)S(1)} %get-tuple-element.16.part_ref, s32[16]{0:T(128)S(1)} %get-tuple-element.17.prev_ref, s32[32]{0:T(128)S(1)} %get-tuple-element.18.last_ref, s32[16]{0:T(128)S(1)} %get-tuple-element.19.tid_ref, ...), custom_call_target="tpu_custom_call" | custom-call | tf_op jit(solution)/shard_map/merge_mirrors/pallas_call | solution.py:660
  133.0 0.6 copy.15
  133.7 1.0 copy.16
Async XLA Ops:
  0.6 47.9 %copy-start = (bf16[128,256]{1,0:T(8,128)(2,1)S(1)}, bf16[128,256]{1,0:T(8,128)(2,1)}, u32[]{:S(2)}) copy-start(bf16[128,256]{1,0:T(8,128)(2,1)} %g_any.3) | copy-start | bytes 196612
  0.6 47.9 %copy-start.1 = (bf16[256,256]{1,0:T(8,128)(2,1)S(1)}, bf16[256,256]{1,0:T(8,128)(2,1)}, u32[]{:S(2)}) copy-start(bf16[256,256]{1,0:T(8,128)(2,1)} %w_any.3) | copy-start | bytes 393220
